TPU v7x, 32 devices: a whole 2x2x4 slice. The times are simulated.
32 devices in a mesh: ctx: 4 (over y, core), tp: 2 (over x), dp: 4 (over z).
Axes of the slice: x: 2, y: 2, z: 4, core: 2. Of those that a mesh axis runs over, the one named last changes fastest.
Arguments:
- queries: bfloat16 [4, 512, 8192], P('dp', 'ctx', 'tp'), may hold values from -6 to 6
- keys: bfloat16 [4, 512, 8192], P('dp', 'ctx', 'tp'), may hold values from -6 to 6
- values: bfloat16 [4, 512, 8192], P('dp', 'ctx', 'tp'), may hold values from -6 to 6
- rates: float32 [8192, 16], P(('tp', 'dp')), may hold values from 0.0001953125 to 0.1
- residues: float32 [8192, 16], P(('tp', 'dp')), may hold values from -1.5 to 1.5
- skip: float32 [8192], P(('tp', 'dp')), may hold values from -3 to 3
Outputs:
- gated: bfloat16 [4, 512, 8192], P('dp', 'ctx', 'tp')
All inputs are finite; a program needn't handle non-finite values.
Results may differ from a plain program's by a relative error of at most 0.015.
Values may be sent and summed in bfloat16 or wider, within the bound.
A program may use at most 64 MiB of HBM per device.

v0:
```python
import math

import jax
import jax.numpy as jnp
from jax import lax
from jax.sharding import PartitionSpec as P

HIGHEST = lax.Precision.HIGHEST


def cos_sin(left_index, right_index, period):
    wrapped = left_index * right_index % period
    angle = 2.0 * math.pi / period * wrapped.astype(jnp.float32)
    return (jnp.cos(angle), jnp.sin(angle))


def counter(count):
    return jnp.arange(count, dtype=jnp.int32)


def spectrum(frequency, rate_modes, residue_modes, length):
    padded = 2 * length
    freq_float = frequency.astype(jnp.float32)
    half_sine = jnp.sin(math.pi / padded * freq_float)
    full_sine = jnp.sin(2.0 * math.pi / padded * freq_float)
    even_index = frequency % 2 == 0
    spec_real = 0.0
    spec_imag = 0.0
    for mode_index in range(rate_modes.shape[0]):
        decay_rate = rate_modes[mode_index]
        residue = residue_modes[mode_index]
        damping = jnp.exp(-decay_rate)
        numerator = jnp.where(
            even_index, -jnp.expm1(-decay_rate * length), 1.0 + jnp.exp(-decay_rate * length)
        )
        denom_real = -jnp.expm1(-decay_rate) + 2.0 * damping * half_sine * half_sine
        denom_imag = damping * full_sine
        factor = (
            residue
            * jnp.sqrt(2.0 * decay_rate)
            * numerator
            / (denom_real * denom_real + denom_imag * denom_imag)
        )
        spec_real = spec_real + factor * denom_real
        spec_imag = spec_imag - factor * denom_imag
    return (spec_real, spec_imag)


def frequency_path(source, rates, residues, ctx_size, position):
    tok_rows, channels = source.shape
    block_rows = tok_rows // ctx_size
    length = tok_rows * ctx_size
    padded = 2 * length
    spread = lax.all_to_all(source[None], "ctx", split_axis=1, concat_axis=0, tiled=True)
    flattened = spread.astype(jnp.float32).reshape(ctx_size, block_rows * channels)
    outer_cos, outer_sin = cos_sin(
        counter(2 * ctx_size)[:, None], counter(ctx_size)[None, :], 2 * ctx_size
    )
    part_real = jnp.dot(outer_cos, flattened, precision=HIGHEST).reshape(
        2 * ctx_size, block_rows, channels
    )
    part_imag = -jnp.dot(outer_sin, flattened, precision=HIGHEST).reshape(
        2 * ctx_size, block_rows, channels
    )
    local_rows = position * block_rows + counter(block_rows)
    twist_cos, twist_sin = cos_sin(counter(2 * ctx_size)[:, None], local_rows[None, :], padded)
    twist_cos = twist_cos[:, :, None]
    twist_sin = twist_sin[:, :, None]
    turned_real = part_real * twist_cos + part_imag * twist_sin
    turned_imag = part_imag * twist_cos - part_real * twist_sin
    moved_real, moved_imag = (
        lax.all_to_all(
            turned_real.astype(jnp.bfloat16), "ctx", split_axis=0, concat_axis=1, tiled=True
        ).astype(turned_real.dtype),
        lax.all_to_all(
            turned_imag.astype(jnp.bfloat16), "ctx", split_axis=0, concat_axis=1, tiled=True
        ).astype(turned_imag.dtype),
    )
    inner_cos, inner_sin = cos_sin(counter(tok_rows)[:, None], counter(tok_rows)[None, :], tok_rows)
    spec_real = jnp.einsum("kt,atc->akc", inner_cos, moved_real, precision=HIGHEST) + jnp.einsum(
        "kt,atc->akc", inner_sin, moved_imag, precision=HIGHEST
    )
    spec_imag = jnp.einsum("kt,atc->akc", inner_cos, moved_imag, precision=HIGHEST) - jnp.einsum(
        "kt,atc->akc", inner_sin, moved_real, precision=HIGHEST
    )
    outer_index = 2 * position + counter(2)
    frequency = outer_index[:, None, None] + 2 * ctx_size * counter(tok_rows)[None, :, None]
    filter_real, filter_imag = spectrum(
        frequency, rates.T[:, None, None, :], residues.T[:, None, None, :], length
    )
    prod_real = spec_real * filter_real - spec_imag * filter_imag
    prod_imag = spec_real * filter_imag + spec_imag * filter_real
    back_real = jnp.einsum("kt,atc->akc", inner_cos, prod_real, precision=HIGHEST) - jnp.einsum(
        "kt,atc->akc", inner_sin, prod_imag, precision=HIGHEST
    )
    back_imag = jnp.einsum("kt,atc->akc", inner_cos, prod_imag, precision=HIGHEST) + jnp.einsum(
        "kt,atc->akc", inner_sin, prod_real, precision=HIGHEST
    )
    back_cos, back_sin = cos_sin(outer_index[:, None], counter(tok_rows)[None, :], padded)
    back_cos = back_cos[:, :, None]
    back_sin = back_sin[:, :, None]
    lifted_real = back_real * back_cos - back_imag * back_sin
    lifted_imag = back_imag * back_cos + back_real * back_sin
    placed_real, placed_imag = (
        lax.all_to_all(
            lifted_real.astype(jnp.bfloat16), "ctx", split_axis=1, concat_axis=0, tiled=True
        ).astype(lifted_real.dtype),
        lax.all_to_all(
            lifted_imag.astype(jnp.bfloat16), "ctx", split_axis=1, concat_axis=0, tiled=True
        ).astype(lifted_imag.dtype),
    )
    final_cos, final_sin = cos_sin(
        counter(ctx_size)[:, None], counter(2 * ctx_size)[None, :], 2 * ctx_size
    )
    series = jnp.dot(
        final_cos, placed_real.reshape(2 * ctx_size, block_rows * channels), precision=HIGHEST
    )
    series = series - jnp.dot(
        final_sin, placed_imag.reshape(2 * ctx_size, block_rows * channels), precision=HIGHEST
    )
    series = (series / padded).reshape(ctx_size, block_rows, channels)
    return lax.all_to_all(
        series.astype(jnp.bfloat16), "ctx", split_axis=0, concat_axis=1, tiled=True
    ).astype(series.dtype)[0]


def body(queries, keys, values, rates, residues, skip):
    rates_all, residues_all, skip_all = (
        lax.all_gather(rates.astype(jnp.bfloat16), "dp", axis=0, tiled=True).astype(rates.dtype),
        lax.all_gather(residues.astype(jnp.bfloat16), "dp", axis=0, tiled=True).astype(
            residues.dtype
        ),
        lax.all_gather(skip.astype(jnp.bfloat16), "dp", axis=0, tiled=True).astype(skip.dtype),
    )
    ctx_size = lax.axis_size("ctx")
    position = lax.axis_index("ctx")
    mixed = (keys.astype(jnp.float32) * values.astype(jnp.float32)).astype(jnp.bfloat16)
    source = mixed[0]
    convolved = frequency_path(source, rates_all, residues_all, ctx_size, position)
    output_rows = queries[0].astype(jnp.float32) * (
        convolved + skip_all[None, :] * source.astype(jnp.float32)
    )
    results = [output_rows.astype(jnp.bfloat16)]
    return jnp.stack(results)


def solution(mesh):
    in_specs = (
        P("dp", "ctx", "tp"),
        P("dp", "ctx", "tp"),
        P("dp", "ctx", "tp"),
        P(("tp", "dp"), None),
        P(("tp", "dp"), None),
        P(("tp", "dp")),
    )
    out_specs = P("dp", "ctx", "tp")
    return jax.shard_map(body, mesh=mesh, in_specs=in_specs, out_specs=out_specs, check_vma=False)
```

profile of v0, /device:TPU:0, one launch (start us, length us, event | category | flops | bytes accessed | tf_op | source)
XLA Modules:
  0.0 336.8 jit_solution(12284940783967423504)
XLA Ops:
  5.6 6.9 %reduce.2 = bf16[128,4096]{1,0:T(8,128)(2,1)S(1)} reduce(bf16[128,1,4096]{2,1,0:T(2,128)(2,1)S(1)} %bitcast.182, bf16[]{:T(256)} %broadcast.860), dimensions={1}, to_apply=%bitcast.173.reduce_sub_computation | reduce | bytes 2097154
  14.6 4.2 %all-to-all-start = ((bf16[4,2,65536]{2,1,0:T(2,128)(2,1)}), bf16[4,2,65536]{2,1,0:T(2,128)(2,1)S(1)}, u32[]{:S(2)}, u32[]{:S(2)}) async-start(bf16[4,2,65536]{2,1,0:T(2,128)(2,1)} %reshape.1442), calls=%async_computation | async-start | bytes 2097152 | tf_op jit(solution)/shard_map/all_to_all | solution.py:54
  18.8 14.3 %all_gather.10 = bf16[4096,16]{0,1:T(8,128)(2,1)S(1)} all-gather(bf16[1024,16]{0,1:T(8,128)(2,1)S(1)} %convert_element_type.149), channel_id=1, replica_groups=mesh['ctx'=4,'tp'=2,'dp'=4] {'dp'}, dimensions={0}, use_global_device_ids=true | all-gather | bytes 163840 | tf_op jit(solution)/shard_map/all_gather | solution.py:129
  38.4 13.6 %all_gather.9 = bf16[4096,16]{0,1:T(8,128)(2,1)S(1)} all-gather(bf16[1024,16]{0,1:T(8,128)(2,1)S(1)} %convert_element_type.148), channel_id=1, replica_groups=mesh['ctx'=4,'tp'=2,'dp'=4] {'dp'}, dimensions={0}, use_global_device_ids=true | all-gather | bytes 163840 | tf_op jit(solution)/shard_map/all_gather | solution.py:130
  58.4 6.2 %bitcast_reduce_fusion = bf16[128,4096]{1,0:T(8,128)(2,1)S(1)} fusion(bf16[128,1,4096]{2,1,0:T(2,128)(2,1)S(1)} %reshape.1443), kind=kLoop, calls=%fused_computation.358 | loop fusion | bytes 2097152 | tf_op jit(solution)/shard_map/all_to_all | solution.py:54
  67.7 15.2 %add_convert_fusion.1 = (bf16[8,32,4096]{2,0,1:T(8,128)(2,1)S(1)}, bf16[8,32,4096]{2,0,1:T(8,128)(2,1)}) fusion(f32[8,32,4096]{2,0,1:T(8,128)S(1)} %fusion.99, f32[8,32]{0,1:T(8,128)S(1)} %get-tuple-element.98, f32[8,32]{0,1:T(8,128)S(1)} %get-tuple-element.97, bf16[32,4096,4]{1,2,0:T(4,128)(2,1)S(1)} %bitcast.180), kind=kOutput, calls=%fused_computation.112 | convolution fusion | flops 59769280 | bytes 9439232 | tf_op jit(solution)/shard_map/dot_general | solution.py:62
  89.8 4.1 %copy.39 = bf16[8,32,4096]{2,1,0:T(8,128)(2,1)} copy(bf16[8,32,4096]{2,0,1:T(8,128)(2,1)} %get-tuple-element.9) | data formatting | bytes 4194304 | tf_op jit(solution)/shard_map/convert_element_type | solution.py:76
  93.9 20.9 %all-to-all-done.1 = bf16[8,32,4096]{2,1,0:T(8,128)(2,1)S(1)} async-done(((bf16[8,32,4096]{2,1,0:T(8,128)(2,1)}), bf16[8,32,4096]{2,1,0:T(8,128)(2,1)S(1)}, u32[]{:S(2)}, u32[]{:S(2)}) %all-to-all-start.1) | async-done | bytes 2097184 | tf_op jit(solution)/shard_map/all_to_all | solution.py:72
  114.8 4.5 %all-to-all-start.2 = ((bf16[8,32,4096]{2,1,0:T(8,128)(2,1)}), bf16[8,32,4096]{2,1,0:T(8,128)(2,1)}, u32[]{:S(2)}, u32[]{:S(2)}) async-start(bf16[8,32,4096]{2,1,0:T(8,128)(2,1)} %copy.39), calls=%async_computation.2 | async-start | bytes 4194304 | tf_op jit(solution)/shard_map/all_to_all | solution.py:75
  122.6 4.2 %fusion.69 = f32[2,4096,128]{2,1,0:T(8,128)} fusion(bf16[2,128,4096]{2,1,0:T(8,128)(2,1)S(1)} %bitcast.177), kind=kOutput, calls=%fused_computation.138 | convolution fusion | flops 1610842112 | bytes 6291456 | tf_op jit(solution)/shard_map/kt,atc->akc/dot_general | solution.py:80
  126.7 18.3 %all-to-all-done.2 = bf16[8,32,4096]{2,1,0:T(8,128)(2,1)} async-done(((bf16[8,32,4096]{2,1,0:T(8,128)(2,1)}), bf16[8,32,4096]{2,1,0:T(8,128)(2,1)}, u32[]{:S(2)}, u32[]{:S(2)}) %all-to-all-start.2) | async-done | bytes 2097184 | tf_op jit(solution)/shard_map/all_to_all | solution.py:75
  153.1 66.9 %multiply_subtract_fusion = (f32[2,128,4096]{1,2,0:T(8,128)S(1)}, f32[2,128,4096]{1,2,0:T(8,128)}, f32[2,128,4096]{1,2,0:T(8,128)}, f32[2,128,4096]{1,2,0:T(8,128)}) fusion(f32[2,128,4096]{1,2,0:T(8,128)S(1)} %fusion.3, f32[4096]{0:T(1024)S(1)} %bitcast.192, f32[4096]{0:T(1024)S(1)} %copy-done.52, f32[4096]{0:T(1024)S(1)} %bitcast.258, ...), kind=kOutput, calls=%fused_computation.93 | convolution fusion | flops 1848639488 | bytes 28903680 | tf_op jit(solution)/shard_map/kt,atc->akc/dot_general | solution.py:83
  220.0 6.6 %multiply_add_fusion = f32[2,128,4096]{1,2,0:T(8,128)S(1)} fusion(f32[2,128,4096]{1,2,0:T(8,128)} %get-tuple-element.99, f32[2,128,4096]{1,2,0:T(8,128)} %get-tuple-element.7, f32[2,128,4096]{1,2,0:T(8,128)} %copy-done, f32[2,128,4096]{1,2,0:T(8,128)} %get-tuple-element.6), kind=kLoop, calls=%fused_computation.92 | loop fusion | flops 3145728 | bytes 20971520 | tf_op jit(solution)/shard_map/add | solution.py:92
  226.6 3.8 %fusion.63 = f32[2,4096,128]{2,1,0:T(8,128)S(1)} fusion(f32[2,128,4096]{1,2,0:T(8,128)S(1)} %multiply_add_fusion), kind=kOutput, calls=%fused_computation.132 | convolution fusion | flops 1610842112 | bytes 8388608 | tf_op jit(solution)/shard_map/kt,atc->akc/dot_general | solution.py:96
  230.4 3.9 %fusion.65 = f32[2,4096,128]{2,1,0:T(8,128)S(1)} fusion(f32[2,128,4096]{1,2,0:T(8,128)S(1)} %get-tuple-element.5), kind=kOutput, calls=%fused_computation.134 | convolution fusion | flops 1610842112 | bytes 8388608 | tf_op jit(solution)/shard_map/kt,atc->akc/dot_general | solution.py:93
  234.3 4.2 %convolution_add_fusion = f32[2,4096,128]{2,1,0:T(8,128)S(1)} fusion(f32[2,4096,128]{2,1,0:T(8,128)S(1)} %fusion.63, f32[2,128,4096]{1,2,0:T(8,128)S(1)} %get-tuple-element.5), kind=kOutput, calls=%fused_computation.35 | convolution fusion | flops 1611890688 | bytes 12582912 | tf_op jit(solution)/shard_map/kt,atc->akc/dot_general | solution.py:96
  238.6 6.0 %fusion.53 = (bf16[2,128,4096]{1,2,0:T(8,128)(2,1)S(1)}, bf16[2,128,4096]{1,2,0:T(8,128)(2,1)}) fusion(f32[2,4096,128]{2,1,0:T(8,128)S(1)} %convolution_add_fusion, f32[2,128]{1,0:T(2,128)S(1)} %copy-done.59, f32[2,128]{1,0:T(2,128)S(1)} %copy-done.58, f32[2,4096,128]{2,1,0:T(8,128)S(1)} %fusion.65, f32[2,128,4096]{1,2,0:T(8,128)S(1)} %multiply_add_fusion), kind=kOutput, calls=%fused_computation.114 | convolution fusion | flops 1620279296 | bytes 16779264 | tf_op jit(solution)/shard_map/kt,atc->akc/dot_general | solution.py:93
  244.6 6.3 %copy.44 = bf16[2,128,4096]{2,0,1:T(2,128)(2,1)} copy(bf16[2,128,4096]{1,2,0:T(8,128)(2,1)} %get-tuple-element.11) | data formatting | bytes 4194304 | tf_op jit(solution)/shard_map/convert_element_type | solution.py:106
  250.9 4.5 %all-to-all-start.3 = ((bf16[2,128,4096]{2,0,1:T(2,128)(2,1)}), bf16[2,128,4096]{2,0,1:T(2,128)(2,1)}, u32[]{:S(2)}, u32[]{:S(2)}) async-start(bf16[2,128,4096]{2,0,1:T(2,128)(2,1)} %copy.44), calls=%async_computation.3 | async-start | bytes 4194304 | tf_op jit(solution)/shard_map/all_to_all | solution.py:105
  255.4 4.0 %copy.47 = bf16[2,128,4096]{2,0,1:T(2,128)(2,1)} copy(bf16[2,128,4096]{1,2,0:T(8,128)(2,1)S(1)} %get-tuple-element.10) | data formatting | bytes 4194304 | tf_op jit(solution)/shard_map/convert_element_type | solution.py:109
  259.4 21.8 %all-to-all-done.3 = bf16[2,128,4096]{2,0,1:T(2,128)(2,1)} async-done(((bf16[2,128,4096]{2,0,1:T(2,128)(2,1)}), bf16[2,128,4096]{2,0,1:T(2,128)(2,1)}, u32[]{:S(2)}, u32[]{:S(2)}) %all-to-all-start.3) | async-done | bytes 2097184 | tf_op jit(solution)/shard_map/all_to_all | solution.py:105
  281.1 3.6 %all-to-all-start.4 = ((bf16[2,128,4096]{2,0,1:T(2,128)(2,1)}), bf16[2,128,4096]{2,0,1:T(2,128)(2,1)S(1)}, u32[]{:S(2)}, u32[]{:S(2)}) async-start(bf16[2,128,4096]{2,0,1:T(2,128)(2,1)} %copy.47), calls=%async_computation.4 | async-start | bytes 4194304 | tf_op jit(solution)/shard_map/all_to_all | solution.py:108
  292.2 18.2 %all-to-all-done.4 = bf16[2,128,4096]{2,0,1:T(2,128)(2,1)S(1)} async-done(((bf16[2,128,4096]{2,0,1:T(2,128)(2,1)}), bf16[2,128,4096]{2,0,1:T(2,128)(2,1)S(1)}, u32[]{:S(2)}, u32[]{:S(2)}) %all-to-all-start.4) | async-done | bytes 2097184 | tf_op jit(solution)/shard_map/all_to_all | solution.py:108
  320.8 11.9 %all_gather.11 = bf16[4096]{0:T(1024)(128)(2,1)S(1)} all-gather(bf16[1024]{0:T(1024)(128)(2,1)S(1)} %convert_element_type.160), channel_id=1, replica_groups=mesh['ctx'=4,'tp'=2,'dp'=4] {'dp'}, dimensions={0}, use_global_device_ids=true | all-gather | bytes 10240 | tf_op jit(solution)/shard_map/all_gather | solution.py:133
  (175 shorter events, 61.4 us)
Async XLA Ops:
  5.1 13.7 %copy-start.18 = (f32[1024,16]{0,1:T(8,128)S(1)}, f32[1024,16]{0,1:T(8,128)}, u32[]{:S(2)}) copy-start(f32[1024,16]{0,1:T(8,128)} %param.9) | copy-start | bytes 196612
  12.6 25.8 %copy-start.19 = (f32[1024,16]{0,1:T(8,128)S(1)}, f32[1024,16]{0,1:T(8,128)}, u32[]{:S(2)}) copy-start(f32[1024,16]{0,1:T(8,128)} %param.10) | copy-start | bytes 196612
  14.6 42.6 %all-to-all-start = ((bf16[4,2,65536]{2,1,0:T(2,128)(2,1)}), bf16[4,2,65536]{2,1,0:T(2,128)(2,1)S(1)}, u32[]{:S(2)}, u32[]{:S(2)}) async-start(bf16[4,2,65536]{2,1,0:T(2,128)(2,1)} %reshape.1442), calls=%async_computation | async-start | bytes 2097152 | tf_op jit(solution)/shard_map/all_to_all | solution.py:54
  35.5 21.6 %copy-start.8 = (f32[1,4096]{1,0:T(1,128)}, f32[1,4096]{1,0:T(1,128)S(1)}, u32[]{:S(2)}) copy-start(f32[1,4096]{1,0:T(1,128)S(1)} %get-tuple-element.52) | copy-start | bytes 49156
  35.5 21.6 %copy-start.10 = (f32[1,4096]{1,0:T(1,128)}, f32[1,4096]{1,0:T(1,128)S(1)}, u32[]{:S(2)}) copy-start(f32[1,4096]{1,0:T(1,128)S(1)} %get-tuple-element.55) | copy-start | bytes 49156
  35.5 21.6 %copy-start.12 = (f32[1,4096]{1,0:T(1,128)}, f32[1,4096]{1,0:T(1,128)S(1)}, u32[]{:S(2)}) copy-start(f32[1,4096]{1,0:T(1,128)S(1)} %get-tuple-element.58) | copy-start | bytes 49156
  35.5 21.6 %copy-start.14 = (f32[1,4096]{1,0:T(1,128)}, f32[1,4096]{1,0:T(1,128)S(1)}, u32[]{:S(2)}) copy-start(f32[1,4096]{1,0:T(1,128)S(1)} %get-tuple-element.61) | copy-start | bytes 49156
  35.5 21.6 %copy-start.16 = (f32[1,4096]{1,0:T(1,128)}, f32[1,4096]{1,0:T(1,128)S(1)}, u32[]{:S(2)}) copy-start(f32[1,4096]{1,0:T(1,128)S(1)} %get-tuple-element.64) | copy-start | bytes 49156
  36.8 20.3 %copy-start.20 = (f32[1,4096]{1,0:T(1,128)}, f32[1,4096]{1,0:T(1,128)S(1)}, u32[]{:S(2)}) copy-start(f32[1,4096]{1,0:T(1,128)S(1)} %get-tuple-element.68) | copy-start | bytes 49156
  36.8 20.3 %copy-start.22 = (f32[1,4096]{1,0:T(1,128)}, f32[1,4096]{1,0:T(1,128)S(1)}, u32[]{:S(2)}) copy-start(f32[1,4096]{1,0:T(1,128)S(1)} %get-tuple-element.71) | copy-start | bytes 49156
  83.0 6.2 %copy-start.6 = (f32[16,4096]{1,0:T(8,128)S(1)}, f32[16,4096]{1,0:T(8,128)}, u32[]{:S(2)}) copy-start(f32[16,4096]{1,0:T(8,128)} %convert_bitcast_fusion.1) | copy-start | bytes 786436
  85.5 29.3 %all-to-all-start.1 = ((bf16[8,32,4096]{2,1,0:T(8,128)(2,1)}), bf16[8,32,4096]{2,1,0:T(8,128)(2,1)S(1)}, u32[]{:S(2)}, u32[]{:S(2)}) async-start(bf16[8,32,4096]{2,1,0:T(8,128)(2,1)} %copy.36), calls=%async_computation.1 | async-start | bytes 4194304 | tf_op jit(solution)/shard_map/all_to_all | solution.py:72
  89.7 29.8 %copy-start.24 = (f32[1,4096]{1,0:T(1,128)S(1)}, f32[1,4096]{1,0:T(1,128)}, u32[]{:S(2)}) copy-start(f32[1,4096]{1,0:T(1,128)} %get-tuple-element.74) | copy-start | bytes 49156
  89.8 29.8 %copy-start.25 = (f32[1,4096]{1,0:T(1,128)S(1)}, f32[1,4096]{1,0:T(1,128)}, u32[]{:S(2)}) copy-start(f32[1,4096]{1,0:T(1,128)} %get-tuple-element.76) | copy-start | bytes 49156
  114.8 6.0 %copy-start.4 = (bf16[8,32,4096]{2,1,0:T(8,128)(2,1)}, bf16[8,32,4096]{2,1,0:T(8,128)(2,1)S(1)}, u32[]{:S(2)}) copy-start(bf16[8,32,4096]{2,1,0:T(8,128)(2,1)S(1)} %all-to-all-done.1) | copy-start | bytes 6291460
  114.8 30.2 %all-to-all-start.2 = ((bf16[8,32,4096]{2,1,0:T(8,128)(2,1)}), bf16[8,32,4096]{2,1,0:T(8,128)(2,1)}, u32[]{:S(2)}, u32[]{:S(2)}) async-start(bf16[8,32,4096]{2,1,0:T(8,128)(2,1)} %copy.39), calls=%async_computation.2 | async-start | bytes 4194304 | tf_op jit(solution)/shard_map/all_to_all | solution.py:75
  152.7 67.3 %copy-start = (f32[2,128,4096]{1,2,0:T(8,128)}, f32[2,128,4096]{1,2,0:T(8,128)S(1)}, u32[]{:S(2)}) copy-start(f32[2,128,4096]{1,2,0:T(8,128)S(1)} %fusion.3) | copy-start | bytes 12582916
  234.3 4.2 %copy-start.58 = (f32[2,128]{1,0:T(2,128)S(1)}, f32[2,128]{1,0:T(2,128)}, u32[]{:S(2)}) copy-start(f32[2,128]{1,0:T(2,128)} %get-tuple-element.93) | copy-start | bytes 3076
  250.9 30.2 %all-to-all-start.3 = ((bf16[2,128,4096]{2,0,1:T(2,128)(2,1)}), bf16[2,128,4096]{2,0,1:T(2,128)(2,1)}, u32[]{:S(2)}, u32[]{:S(2)}) async-start(bf16[2,128,4096]{2,0,1:T(2,128)(2,1)} %copy.44), calls=%async_computation.3 | async-start | bytes 4194304 | tf_op jit(solution)/shard_map/all_to_all | solution.py:105
  281.1 29.3 %all-to-all-start.4 = ((bf16[2,128,4096]{2,0,1:T(2,128)(2,1)}), bf16[2,128,4096]{2,0,1:T(2,128)(2,1)S(1)}, u32[]{:S(2)}, u32[]{:S(2)}) async-start(bf16[2,128,4096]{2,0,1:T(2,128)(2,1)} %copy.47), calls=%async_computation.4 | async-start | bytes 4194304 | tf_op jit(solution)/shard_map/all_to_all | solution.py:108
  313.3 7.4 %copy-start.60 = (f32[1024]{0:T(1024)S(1)}, f32[1024]{0:T(1024)}, u32[]{:S(2)}) copy-start(f32[1024]{0:T(1024)} %param.11) | copy-start | bytes 12292
  313.3 21.8 %copy-start.3 = (bf16[1,128,4096]{2,1,0:T(8,128)(2,1)S(1)}, bf16[1,128,4096]{2,1,0:T(8,128)(2,1)}, u32[]{:S(2)}) copy-start(bf16[1,128,4096]{2,1,0:T(8,128)(2,1)} %copy-done.2) | copy-start | bytes 3145732
  313.3 21.8 %copy-start.7 = (bf16[1,128,4096]{2,1,0:T(8,128)(2,1)S(1)}, bf16[1,128,4096]{2,1,0:T(8,128)(2,1)}, u32[]{:S(2)}) copy-start(bf16[1,128,4096]{2,1,0:T(8,128)(2,1)} %param.6) | copy-start | bytes 3145732
  317.2 18.0 %all-to-all-start.5 = ((bf16[4,32,4096]{2,1,0:T(8,128)(2,1)}), bf16[4,32,4096]{2,1,0:T(8,128)(2,1)S(1)}, u32[]{:S(2)}, u32[]{:S(2)}) async-start(bf16[4,32,4096]{2,1,0:T(8,128)(2,1)} %bitcast.172), calls=%async_computation.5 | async-start | bytes 2097152 | tf_op jit(solution)/shard_map/all_to_all | solution.py:122
  (43 other events, 137.4 us)
where the time goes:
time: 341 us; the launch traced here: 337 us
  matrix products  118 us (35%)
  waiting for transfers between devices  81.7 us (24%)
  local copies, waits for them, and re-layouts  43.4 us (13%)
  blocking collectives  39.8 us (12%)
  other arithmetic  29.1 us (9%)
  starting transfers between devices  23.9 us (7%)
    dot_general x1, matrix products, frequency_path(): jnp.einsum('kt,atc->akc', inner_sin, moved_real, precision=HIGHEST)  66.9 us
    all_to_all x1, waiting for transfers between devices, frequency_path(): lax.all_to_all(lifted_real.astype(jnp.bfloat16), 'ctx', split_axis=1, con...  21.8 us
    all_to_all x1, waiting for transfers between devices, frequency_path(): lax.all_to_all(turned_real.astype(jnp.bfloat16), 'ctx', split_axis=0, con...  20.9 us
    all_to_all x1, waiting for transfers between devices, frequency_path(): lax.all_to_all(turned_imag.astype(jnp.bfloat16), 'ctx', split_axis=0, con...  18.3 us
    all_to_all x1, waiting for transfers between devices, frequency_path(): lax.all_to_all(lifted_imag.astype(jnp.bfloat16), 'ctx', split_axis=1, con...  18.2 us
    dot_general x1, matrix products, frequency_path(): jnp.dot(outer_sin, flattened, precision=HIGHEST)  15.2 us
    all_gather x1, blocking collectives, body(): lax.all_gather(rates.astype(jnp.bfloat16), 'dp', axis=0, tiled=True)  14.3 us
    all_gather x1, blocking collectives, body(): lax.all_gather(residues.astype(jnp.bfloat16), 'dp', axis=0, tiled=True)  13.6 us
  transfers between devices with their start and end apart: 6, of which 5 were waited for; matrix products, arithmetic and copies ran while one was open for 10% of the time, Pallas kernels for 0%

commit v1 on v0

v1 whole, which is shorter than its diff:
```python
import functools
import math

import jax
import jax.numpy as jnp
import ml_dtypes
import numpy as np
from jax import lax
from jax.experimental import pallas as pl
from jax.experimental.pallas import tpu as pltpu
from jax.sharding import PartitionSpec as P

MESH = pl.DeviceIdType.MESH
LANES = 128


def transforms(block):
    bins = np.arange(block, dtype=np.int64)
    turns = (2 * bins[:, None] + 1) * bins[None, :] % (4 * block)
    angle = 2.0 * math.pi / (4 * block) * turns
    forward = np.concatenate([np.cos(angle), np.sin(angle)], axis=0)
    inverse = forward.T / block
    return forward.astype(ml_dtypes.bfloat16), inverse.astype(ml_dtypes.bfloat16)


def kernel(
    sizes,
    q_hbm, k_hbm, v_hbm, rates_ref, residues_ref, skip_ref, fwd_hbm, inv_hbm,
    out_hbm,
    kb, vb, mixs, mixf, qf, outb, par, skp, taps, conv, fwd, inv, statef, states, staten,
    in_sem, q_sem, mix_sem, par_send, par_recv, skp_send, skp_recv, st_send, st_recv, out_sem,
):
    tokens, half, shard, modes, ctx_size, dp_size, width = sizes
    pairs = ctx_size // 2
    half_shards = dp_size // 2
    block = 2 * tokens
    chunks = half // width
    groups = width // LANES
    ctx = lax.axis_index("ctx")
    dp = lax.axis_index("dp")
    pos = ctx // 2
    core = ctx % 2
    mate_core = 1 - core
    mate = pos * 2 + mate_core
    my_cols = pl.multiple_of(core * half, LANES)
    mate_cols = pl.multiple_of(mate_core * half, LANES)
    my_rows = pl.ds(pl.multiple_of(core * tokens, 16), tokens)
    mate_rows = pl.ds(pl.multiple_of(mate_core * tokens, 16), tokens)

    load_k = pltpu.make_async_copy(k_hbm, kb, in_sem.at[0])
    load_v = pltpu.make_async_copy(v_hbm, vb, in_sem.at[1])
    load_q = pltpu.make_async_copy(q_hbm.at[:, pl.ds(my_cols, half)], qf.at[my_rows, :], in_sem.at[2])
    load_f = pltpu.make_async_copy(fwd_hbm, fwd, in_sem.at[3])
    load_i = pltpu.make_async_copy(inv_hbm, inv, in_sem.at[4])
    load_k.start()
    load_v.start()
    load_f.start()
    load_i.start()
    load_q.start()

    barrier = pltpu.get_barrier_semaphore()
    pl.semaphore_signal(barrier, inc=1, device_id={"ctx": mate}, device_id_type=MESH)
    for step in range(1, dp_size):
        pl.semaphore_signal(
            barrier, inc=1, device_id={"dp": (dp + step) % dp_size}, device_id_type=MESH
        )
    for step in range(1, pairs):
        pl.semaphore_signal(
            barrier, inc=1, device_id={"ctx": (ctx + 2 * step) % ctx_size}, device_id_type=MESH
        )

    slot = dp % half_shards
    owns = dp // half_shards == core

    @pl.when(owns)
    def _():
        decay = rates_ref[...]
        par[slot, 0] = decay.astype(jnp.bfloat16)
        par[slot, 1] = (residues_ref[...] * jnp.sqrt(2.0 * decay)).astype(jnp.bfloat16)
        skp[slot] = skip_ref[...]

    pl.semaphore_wait(barrier, 1 + (dp_size - 1) + (pairs - 1))

    def par_copy(place, target, lane):
        return pltpu.make_async_remote_copy(
            src_ref=par.at[place], dst_ref=par.at[place], send_sem=par_send.at[lane],
            recv_sem=par_recv.at[place], device_id={"dp": target}, device_id_type=MESH,
        )

    def skp_copy(place, target, lane):
        return pltpu.make_async_remote_copy(
            src_ref=skp.at[place], dst_ref=skp.at[place], send_sem=skp_send.at[lane],
            recv_sem=skp_recv.at[place], device_id={"dp": target}, device_id_type=MESH,
        )

    @pl.when(owns)
    def _():
        for step in range(1, dp_size):
            target = (dp + step) % dp_size
            par_copy(slot, target, step - 1).start()
            skp_copy(slot, target, step - 1).start()

    send_q = pltpu.make_async_remote_copy(
        src_ref=q_hbm.at[:, pl.ds(mate_cols, half)], dst_ref=qf.at[my_rows, :],
        send_sem=q_sem.at[0], recv_sem=q_sem.at[1], device_id={"ctx": mate}, device_id_type=MESH,
    )
    send_mix = pltpu.make_async_remote_copy(
        src_ref=mixs, dst_ref=mixf.at[my_rows, :],
        send_sem=mix_sem.at[0], recv_sem=mix_sem.at[1], device_id={"ctx": mate}, device_id_type=MESH,
    )

    load_k.wait()
    load_v.wait()

    @pl.loop(0, chunks)
    def _(index):
        dst = pl.ds(pl.multiple_of(index * width, LANES), width)
        src = pl.ds(pl.multiple_of(mate_cols + index * width, LANES), width)
        mixs[:, dst] = (
            kb[:, src].astype(jnp.float32) * vb[:, src].astype(jnp.float32)
        ).astype(jnp.bfloat16)

    send_mix.start()
    send_q.start()

    @pl.loop(0, chunks)
    def _(index):
        dst = pl.ds(pl.multiple_of(index * width, LANES), width)
        src = pl.ds(pl.multiple_of(my_cols + index * width, LANES), width)
        mixf[my_rows, dst] = (
            kb[:, src].astype(jnp.float32) * vb[:, src].astype(jnp.float32)
        ).astype(jnp.bfloat16)

    for place in range(half_shards):
        source = core * half_shards + place

        @pl.when(source != dp)
        def _():
            par_copy(place, source, 0).wait_recv()
            skp_copy(place, source, 0).wait_recv()

    send_mix.wait_recv()

    shard_groups = shard // LANES
    rows8 = lax.broadcasted_iota(jnp.int32, (8, LANES), 0).astype(jnp.float32)

    def spread(row):
        return jnp.broadcast_to(row, (8, LANES))

    def group_params(group):
        place = group // shard_groups
        cols = pl.ds(pl.multiple_of(group % shard_groups * LANES, LANES), LANES)
        return (
            par[place, 0, :, cols].astype(jnp.float32),
            par[place, 1, :, cols].astype(jnp.float32),
        )

    def tree(parts):
        while len(parts) > 1:
            parts = [
                parts[i] + parts[i + 1] if i + 1 < len(parts) else parts[i]
                for i in range(0, len(parts), 2)
            ]
        return parts[0]

    def exp_sums(decay, start, store):
        ratio = jnp.exp(-8.0 * decay)
        ratios = [spread(ratio[m : m + 1]) for m in range(modes)]

        def step(index, powers):
            first = tree(list(powers))
            powers = [p * a for p, a in zip(powers, ratios)]
            second = tree(powers)
            store(pl.multiple_of(index * 16, 16), jnp.concatenate([first, second], axis=0))
            return tuple(p * a for p, a in zip(powers, ratios))

        powers = tuple(
            spread(start[m : m + 1]) * jnp.exp(-spread(decay[m : m + 1]) * rows8)
            for m in range(modes)
        )
        lax.fori_loop(0, block // 16, step, powers)

    def state_copy(index, target_pos, source_pos):
        cols = pl.ds(pl.multiple_of(index * width, LANES), width)
        return pltpu.make_async_remote_copy(
            src_ref=states.at[:, cols], dst_ref=staten.at[source_pos, :, cols],
            send_sem=st_send.at[target_pos, index], recv_sem=st_recv.at[source_pos, index],
            device_id={"ctx": target_pos * 2 + core}, device_id_type=MESH,
        )

    if pairs > 1:

        @pl.when(pos < pairs - 1)
        def _():
            @pl.loop(0, chunks)
            def _(index):
                @pl.loop(0, groups)
                def _(inner):
                    group = index * groups + inner
                    cols = pl.ds(pl.multiple_of(group * LANES, LANES), LANES)
                    decay, _ = group_params(group)
                    ratio = jnp.exp(-8.0 * decay)
                    ratios = [spread(ratio[m : m + 1]) for m in range(modes)]

                    def step(row, held):
                        both = mixf[pl.ds(pl.multiple_of(row * 16, 16), 16), cols].astype(jnp.float32)
                        held = [h * a + both[0:8] for h, a in zip(held, ratios)]
                        return tuple(h * a + both[8:16] for h, a in zip(held, ratios))

                    held = tuple(jnp.zeros((8, LANES), jnp.float32) for _ in range(modes))
                    held = lax.fori_loop(0, block // 16, step, held)
                    for m in range(modes):
                        last = held[m] * jnp.exp(-spread(decay[m : m + 1]) * (7.0 - rows8))
                        statef[m : m + 1, :] = jnp.sum(last, axis=0, keepdims=True)
                    states[:, cols] = statef[...].astype(jnp.bfloat16)

                for later in range(1, pairs):

                    @pl.when(pos < later)
                    def _():
                        state_copy(index, later, pos).start()

    load_f.wait()
    load_i.wait()

    @pl.loop(0, chunks)
    def _(index):
        @pl.loop(0, groups)
        def _(inner):
            group = index * groups + inner
            cols = pl.ds(pl.multiple_of(group * LANES, LANES), LANES)
            decay, gain = group_params(group)

            def store(row, sums):
                taps[pl.ds(row, 16), pl.ds(pl.multiple_of(inner * LANES, LANES), LANES)] = sums.astype(
                    jnp.bfloat16
                )

            exp_sums(decay, gain, store)

        cols = pl.ds(pl.multiple_of(index * width, LANES), width)
        forward = fwd[...]
        spec = jnp.dot(forward, mixf[:, cols], preferred_element_type=jnp.float32)
        filt = jnp.dot(forward, taps[...], preferred_element_type=jnp.float32)
        sr, si = spec[:block], spec[block:]
        fr, fi = filt[:block], filt[block:]
        prod_r = (sr * fr - si * fi).astype(jnp.bfloat16)
        prod_i = (sr * fi + si * fr).astype(jnp.bfloat16)
        conv[:, cols] = jnp.dot(
            inv[:, :block], prod_r, preferred_element_type=jnp.float32
        ) + jnp.dot(inv[:, block:], prod_i, preferred_element_type=jnp.float32)

    load_q.wait()
    send_q.wait_recv()

    def out_copies(index):
        cols = pl.ds(pl.multiple_of(index * width, LANES), width)
        target = pl.ds(pl.multiple_of(my_cols + index * width, LANES), width)
        local = pltpu.make_async_copy(
            outb.at[my_rows, cols], out_hbm.at[:, target], out_sem.at[0, index]
        )
        remote = pltpu.make_async_remote_copy(
            src_ref=outb.at[mate_rows, cols], dst_ref=out_hbm.at[:, target],
            send_sem=out_sem.at[1, index], recv_sem=out_sem.at[2, index],
            device_id={"ctx": mate}, device_id_type=MESH,
        )
        return local, remote

    @pl.loop(0, chunks)
    def _(index):
        for earlier in range(pairs - 1):

            @pl.when(earlier < pos)
            def _():
                state_copy(index, pos, earlier).wait_recv()

        @pl.when(pos > 0)
        def _():
            @pl.loop(0, groups)
            def _(inner):
                group = index * groups + inner
                cols = pl.ds(pl.multiple_of(group * LANES, LANES), LANES)
                decay, gain = group_params(group)
                across = jnp.exp(-float(block) * decay)
                total = jnp.zeros((modes, LANES), jnp.float32)
                for earlier in range(pairs - 1):
                    total = jnp.where(
                        earlier < pos,
                        total * across + staten[earlier, :, cols].astype(jnp.float32),
                        total,
                    )
                start = total * gain * jnp.exp(-decay)

                def store(row, sums):
                    conv[pl.ds(row, 16), cols] += sums

                exp_sums(decay, start, store)

        @pl.loop(0, groups)
        def _(inner):
            group = index * groups + inner
            cols = pl.ds(pl.multiple_of(group * LANES, LANES), LANES)
            place = group // shard_groups
            direct = skp[place, :, pl.ds(pl.multiple_of(group % shard_groups * LANES, LANES), LANES)]
            outb[:, cols] = (
                qf[:, cols].astype(jnp.float32)
                * (conv[:, cols] + direct * mixf[:, cols].astype(jnp.float32))
            ).astype(jnp.bfloat16)

        local, remote = out_copies(index)
        local.start()
        remote.start()

    @pl.when(owns)
    def _():
        for step in range(1, dp_size):
            target = (dp + step) % dp_size
            par_copy(slot, target, step - 1).wait_send()
            skp_copy(slot, target, step - 1).wait_send()

    send_q.wait_send()
    send_mix.wait_send()
    for index in range(chunks):
        for later in range(1, pairs):

            @pl.when(pos < later)
            def _():
                state_copy(index, later, pos).wait_send()

        local, remote = out_copies(index)
        local.wait()
        remote.wait()


def body(queries, keys, values, rates, residues, skip):
    tokens, channels = queries.shape[1:]
    shard, modes = rates.shape
    ctx_size = lax.axis_size("ctx")
    dp_size = lax.axis_size("dp")
    pairs = ctx_size // 2
    half = channels // 2
    block = 2 * tokens
    width = min(512, half)
    chunks = half // width
    forward, inverse = transforms(block)
    any_spec = pl.BlockSpec(memory_space=pl.ANY)
    vmem_spec = pl.BlockSpec(memory_space=pltpu.VMEM)
    bf16, f32 = jnp.bfloat16, jnp.float32
    slots = max(pairs - 1, 1)
    dma = pltpu.SemaphoreType.DMA
    sizes = (tokens, half, shard, modes, ctx_size, dp_size, width)
    gated = pl.pallas_call(
        functools.partial(kernel, sizes),
        out_shape=jax.ShapeDtypeStruct((tokens, channels), bf16),
        in_specs=[any_spec] * 3 + [vmem_spec] * 3 + [any_spec] * 2,
        out_specs=any_spec,
        scratch_shapes=[
            pltpu.VMEM((tokens, channels), bf16),
            pltpu.VMEM((tokens, channels), bf16),
            pltpu.VMEM((tokens, half), bf16),
            pltpu.VMEM((block, half), bf16),
            pltpu.VMEM((block, half), bf16),
            pltpu.VMEM((block, half), bf16),
            pltpu.VMEM((dp_size // 2, 2, modes, shard), bf16),
            pltpu.VMEM((dp_size // 2, 1, shard), f32),
            pltpu.VMEM((block, width), bf16),
            pltpu.VMEM((block, half), f32),
            pltpu.VMEM((2 * block, block), bf16),
            pltpu.VMEM((block, 2 * block), bf16),
            pltpu.VMEM((modes, LANES), f32),
            pltpu.VMEM((modes, half), bf16),
            pltpu.VMEM((slots, modes, half), bf16),
            dma((5,)),
            dma((2,)),
            dma((2,)),
            dma((dp_size - 1,)),
            dma((dp_size // 2,)),
            dma((dp_size - 1,)),
            dma((dp_size // 2,)),
            dma((pairs, chunks)),
            dma((slots, chunks)),
            dma((3, chunks)),
        ],
        compiler_params=pltpu.CompilerParams(
            collective_id=0, has_side_effects=True, vmem_limit_bytes=40 * 2**20
        ),
    )(
        queries[0], keys[0], values[0], rates.T, residues.T, skip[None, :],
        jnp.asarray(forward), jnp.asarray(inverse),
    )
    return gated[None]


def solution(mesh):
    in_specs = (
        P("dp", "ctx", "tp"),
        P("dp", "ctx", "tp"),
        P("dp", "ctx", "tp"),
        P(("tp", "dp"), None),
        P(("tp", "dp"), None),
        P(("tp", "dp")),
    )
    out_specs = P("dp", "ctx", "tp")
    return jax.shard_map(body, mesh=mesh, in_specs=in_specs, out_specs=out_specs, check_vma=False)
```

time: 341 us -> 31.8 us (0.09); the launches traced: 337 us -> 31.4 us
  matrix products: 118 us -> 0 us
  waiting for transfers between devices: 81.7 us -> 0 us
  blocking collectives: 39.8 us -> 0 us
  local copies, waits for them, and re-layouts: 43.4 us -> 8.91 us
  other arithmetic: 29.1 us -> 0 us
  starting transfers between devices: 23.9 us -> 0 us
  Pallas kernels: 0 us -> 22.5 us
    dot_general x12 -> x0, matrix products: 118 us -> none  [the longest x1 66.9 us: frequency_path(): jnp.einsum('kt,atc->akc', inner_sin, moved_real, precision=HIGHEST)]
    all_to_all x6 -> x0, waiting for transfers between devices: 81.7 us -> none  [the longest x1 21.8 us: frequency_path(): lax.all_to_all(lifted_real.astype(jnp.bfloat16), 'ctx', split_axis=1, con...]
    all_gather x3 -> x0, blocking collectives: 39.8 us -> none  [the longest x1 14.3 us: body(): lax.all_gather(rates.astype(jnp.bfloat16), 'dp', axis=0, tiled=True)]
    all_to_all x6 -> x0, starting transfers between devices: 23.9 us -> none  [the longest x1 4.46 us: frequency_path(): lax.all_to_all(lifted_real.astype(jnp.bfloat16), 'ctx', split_axis=1, con...]
    pallas_call x0 -> x1, Pallas kernels: none -> 22.5 us  [body(): pl.pallas_call(functools.partial(kernel, sizes), out_shape=jax.ShapeDtype...]
    convert_element_type x5 -> x0, local copies, waits for them, and re-layouts: 19.3 us -> none  [the longest x1 6.31 us: frequency_path(): lifted_real.astype(jnp.bfloat16)]
    all_to_all x7 -> x0, local copies, waits for them, and re-layouts: 14.4 us -> none  [the longest x1 6.21 us: frequency_path(): lax.all_to_all(source[None], 'ctx', split_axis=1, concat_axis=0, tiled=True)]
    add x4 -> x0, other arithmetic: 7.72 us -> none  [the longest x1 6.58 us: frequency_path(): prod_imag = spec_real * filter_imag + spec_imag * filter_real]
  transfers between devices with their start and end apart: 6 -> 0, of which waited for: 5 -> 0; matrix products, arithmetic and copies ran while one was open for 10% -> 0% of each run, Pallas kernels for 0% -> 0%
where the time goes in v1:
time: 31.8 us; the launch traced here: 31.4 us
  Pallas kernels  22.5 us (71%)
  local copies, waits for them, and re-layouts  8.91 us (28%)
    pallas_call x1, Pallas kernels, body(): pl.pallas_call(functools.partial(kernel, sizes), out_shape=jax.ShapeDtype...  22.5 us
    unnamed x17, local copies, waits for them, and re-layouts  8.91 us

profile of v1, /device:TPU:0, one launch (start us, length us, event | category | flops | bytes accessed | tf_op | source)
XLA Modules:
  0.0 31.4 jit_solution(11331180065918344199)
XLA Ops:
  0.0 0.0 copy-start.7
  0.0 0.7 %copy-done.7 = f32[1024]{0:T(1024)S(1)} copy-done((f32[1024]{0:T(1024)S(1)}, f32[1024]{0:T(1024)}, u32[]{:S(2)}) %copy-start.7) | copy-done | bytes 4120
  0.7 0.0 copy-start
  0.7 1.2 %copy-done = bf16[1,128,4096]{2,1,0:T(8,128)(2,1)S(1)} copy-done((bf16[1,128,4096]{2,1,0:T(8,128)(2,1)S(1)}, bf16[1,128,4096]{2,1,0:T(8,128)(2,1)}, u32[]{:S(2)}) %copy-start) | copy-done | bytes 1048600
  1.9 0.0 copy-start.1
  1.9 1.2 %copy-done.1 = bf16[1,128,4096]{2,1,0:T(8,128)(2,1)S(1)} copy-done((bf16[1,128,4096]{2,1,0:T(8,128)(2,1)S(1)}, bf16[1,128,4096]{2,1,0:T(8,128)(2,1)}, u32[]{:S(2)}) %copy-start.1) | copy-done | bytes 1048600
  3.1 0.0 copy-start.2
  3.1 1.2 %copy-done.2 = bf16[1,128,4096]{2,1,0:T(8,128)(2,1)S(1)} copy-done((bf16[1,128,4096]{2,1,0:T(8,128)(2,1)S(1)}, bf16[1,128,4096]{2,1,0:T(8,128)(2,1)}, u32[]{:S(2)}) %copy-start.2) | copy-done | bytes 1048600
  4.4 0.0 copy-start.3
  4.4 0.9 %copy-done.3 = bf16[256,512]{1,0:T(8,128)(2,1)S(1)} copy-done((bf16[256,512]{1,0:T(8,128)(2,1)S(1)}, bf16[256,512]{1,0:T(8,128)(2,1)}, u32[]{:S(2)}) %copy-start.3) | copy-done | bytes 262168
  5.3 0.0 copy-start.4
  5.3 0.9 %copy-done.4 = bf16[512,256]{1,0:T(8,128)(2,1)S(1)} copy-done((bf16[512,256]{1,0:T(8,128)(2,1)S(1)}, bf16[512,256]{1,0:T(8,128)(2,1)}, u32[]{:S(2)}) %copy-start.4) | copy-done | bytes 262168
  6.3 0.0 copy-start.5
  6.3 0.8 %copy-done.5 = f32[1024,16]{0,1:T(8,128)S(1)} copy-done((f32[1024,16]{0,1:T(8,128)S(1)}, f32[1024,16]{0,1:T(8,128)}, u32[]{:S(2)}) %copy-start.5) | copy-done | bytes 65560
  7.1 0.0 copy-start.6
  7.1 0.8 %copy-done.6 = f32[1024,16]{0,1:T(8,128)S(1)} copy-done((f32[1024,16]{0,1:T(8,128)S(1)}, f32[1024,16]{0,1:T(8,128)}, u32[]{:S(2)}) %copy-start.6) | copy-done | bytes 65560
  7.9 22.5 %shard_map.82 = bf16[128,4096]{1,0:T(8,128)(2,1)S(1)} custom-call(bf16[128,4096]{1,0:T(8,128)(2,1)S(1)} %bitcast.8, bf16[128,4096]{1,0:T(8,128)(2,1)S(1)} %bitcast.9, bf16[128,4096]{1,0:T(8,128)(2,1)S(1)} %bitcast.10, f32[16,1024]{1,0:T(8,128)S(1)} %bitcast.11, f32[16,1024]{1,0:T(8,128)S(1)} %bitcast.12, f32[1,1024]{1,0:T(1,128)S(1)} %bitcast.13, ...), custom_call_target="tpu_custom_call" | custom-call | tf_op jit(solution)/shard_map/pallas_call | solution.py:352
  30.4 1.0 %copy.10 = bf16[1,128,4096]{2,1,0:T(8,128)(2,1)} copy(bf16[1,128,4096]{2,1,0:T(8,128)(2,1)S(1)} %bitcast.7) | data formatting | bytes 2097152
Async XLA Ops:
  0.0 0.7 %copy-start.7 = (f32[1024]{0:T(1024)S(1)}, f32[1024]{0:T(1024)}, u32[]{:S(2)}) copy-start(f32[1024]{0:T(1024)} %param.13) | copy-start | bytes 12292
  0.7 1.2 %copy-start = (bf16[1,128,4096]{2,1,0:T(8,128)(2,1)S(1)}, bf16[1,128,4096]{2,1,0:T(8,128)(2,1)}, u32[]{:S(2)}) copy-start(bf16[1,128,4096]{2,1,0:T(8,128)(2,1)} %param.8) | copy-start | bytes 3145732
  1.9 1.2 %copy-start.1 = (bf16[1,128,4096]{2,1,0:T(8,128)(2,1)S(1)}, bf16[1,128,4096]{2,1,0:T(8,128)(2,1)}, u32[]{:S(2)}) copy-start(bf16[1,128,4096]{2,1,0:T(8,128)(2,1)} %param.9) | copy-start | bytes 3145732
  3.1 1.2 %copy-start.2 = (bf16[1,128,4096]{2,1,0:T(8,128)(2,1)S(1)}, bf16[1,128,4096]{2,1,0:T(8,128)(2,1)}, u32[]{:S(2)}) copy-start(bf16[1,128,4096]{2,1,0:T(8,128)(2,1)} %param.10) | copy-start | bytes 3145732
  4.4 0.9 %copy-start.3 = (bf16[256,512]{1,0:T(8,128)(2,1)S(1)}, bf16[256,512]{1,0:T(8,128)(2,1)}, u32[]{:S(2)}) copy-start(bf16[256,512]{1,0:T(8,128)(2,1)} %constant.5.clone.inv_hbm) | copy-start | bytes 786436
  5.3 0.9 %copy-start.4 = (bf16[512,256]{1,0:T(8,128)(2,1)S(1)}, bf16[512,256]{1,0:T(8,128)(2,1)}, u32[]{:S(2)}) copy-start(bf16[512,256]{1,0:T(8,128)(2,1)} %constant.4.clone.fwd_hbm) | copy-start | bytes 786436
  6.3 0.8 %copy-start.5 = (f32[1024,16]{0,1:T(8,128)S(1)}, f32[1024,16]{0,1:T(8,128)}, u32[]{:S(2)}) copy-start(f32[1024,16]{0,1:T(8,128)} %param.11) | copy-start | bytes 196612
  7.1 0.8 %copy-start.6 = (f32[1024,16]{0,1:T(8,128)S(1)}, f32[1024,16]{0,1:T(8,128)}, u32[]{:S(2)}) copy-start(f32[1024,16]{0,1:T(8,128)} %param.12) | copy-start | bytes 196612

commit v2 on v1

--- a/solution.py
+++ b/solution.py
@@ -25,9 +25,9 @@
 
 def kernel(
     sizes,
-    q_hbm, k_hbm, v_hbm, rates_ref, residues_ref, skip_ref, fwd_hbm, inv_hbm,
+    q_hbm, k_hbm, v_hbm, rates_hbm, residues_hbm, skip_hbm, fwd_hbm, inv_hbm,
     out_hbm,
-    kb, vb, mixs, mixf, qf, outb, par, skp, taps, conv, fwd, inv, statef, states, staten,
+    rates_ref, residues_ref, kb, vb, mixs, mixf, qf, outb, par, skp, taps, conv, fwd, inv, statef, states, staten,
     in_sem, q_sem, mix_sem, par_send, par_recv, skp_send, skp_recv, st_send, st_recv, out_sem,
 ):
     tokens, half, shard, modes, ctx_size, dp_size, width = sizes
@@ -52,6 +52,18 @@
     load_q = pltpu.make_async_copy(q_hbm.at[:, pl.ds(my_cols, half)], qf.at[my_rows, :], in_sem.at[2])
     load_f = pltpu.make_async_copy(fwd_hbm, fwd, in_sem.at[3])
     load_i = pltpu.make_async_copy(inv_hbm, inv, in_sem.at[4])
+    slot = dp % half_shards
+    owns = dp // half_shards == core
+    load_r = pltpu.make_async_copy(rates_hbm, rates_ref, in_sem.at[5])
+    load_g = pltpu.make_async_copy(residues_hbm, residues_ref, in_sem.at[6])
+    load_s = pltpu.make_async_copy(skip_hbm, skp.at[slot], in_sem.at[7])
+
+    @pl.when(owns)
+    def _():
+        load_r.start()
+        load_g.start()
+        load_s.start()
+
     load_k.start()
     load_v.start()
     load_f.start()
@@ -69,15 +81,14 @@
             barrier, inc=1, device_id={"ctx": (ctx + 2 * step) % ctx_size}, device_id_type=MESH
         )
 
-    slot = dp % half_shards
-    owns = dp // half_shards == core
-
     @pl.when(owns)
     def _():
+        load_r.wait()
+        load_g.wait()
+        load_s.wait()
         decay = rates_ref[...]
         par[slot, 0] = decay.astype(jnp.bfloat16)
         par[slot, 1] = (residues_ref[...] * jnp.sqrt(2.0 * decay)).astype(jnp.bfloat16)
-        skp[slot] = skip_ref[...]
 
     pl.semaphore_wait(barrier, 1 + (dp_size - 1) + (pairs - 1))
 
@@ -343,8 +354,7 @@
     width = min(512, half)
     chunks = half // width
     forward, inverse = transforms(block)
-    any_spec = pl.BlockSpec(memory_space=pl.ANY)
-    vmem_spec = pl.BlockSpec(memory_space=pltpu.VMEM)
+    hbm_spec = pl.BlockSpec(memory_space=pltpu.HBM)
     bf16, f32 = jnp.bfloat16, jnp.float32
     slots = max(pairs - 1, 1)
     dma = pltpu.SemaphoreType.DMA
@@ -352,9 +362,11 @@
     gated = pl.pallas_call(
         functools.partial(kernel, sizes),
         out_shape=jax.ShapeDtypeStruct((tokens, channels), bf16),
-        in_specs=[any_spec] * 3 + [vmem_spec] * 3 + [any_spec] * 2,
-        out_specs=any_spec,
+        in_specs=[hbm_spec] * 8,
+        out_specs=hbm_spec,
         scratch_shapes=[
+            pltpu.VMEM((modes, shard), f32),
+            pltpu.VMEM((modes, shard), f32),
             pltpu.VMEM((tokens, channels), bf16),
             pltpu.VMEM((tokens, channels), bf16),
             pltpu.VMEM((tokens, half), bf16),
@@ -370,7 +382,7 @@
             pltpu.VMEM((modes, LANES), f32),
             pltpu.VMEM((modes, half), bf16),
             pltpu.VMEM((slots, modes, half), bf16),
-            dma((5,)),
+            dma((8,)),
             dma((2,)),
             dma((2,)),
             dma((dp_size - 1,)),
@@ -382,7 +394,7 @@
             dma((3, chunks)),
         ],
         compiler_params=pltpu.CompilerParams(
-            collective_id=0, has_side_effects=True, vmem_limit_bytes=40 * 2**20
+            collective_id=0, has_side_effects=True, vmem_limit_bytes=60 * 2**20
         ),
     )(
         queries[0], keys[0], values[0], rates.T, residues.T, skip[None, :],

time: 31.8 us -> 24.7 us (0.78)
  local copies, waits for them, and re-layouts: 8.91 us -> 2.29 us
    unnamed x17 -> x1, local copies, waits for them, and re-layouts: 8.91 us -> 2.29 us
where the time goes in v2:
time: 24.7 us; the launch traced here: 24.6 us
  Pallas kernels  22.3 us (90%)
  local copies, waits for them, and re-layouts  2.29 us (9%)
    pallas_call x1, Pallas kernels, body(): pl.pallas_call(functools.partial(kernel, sizes), out_shape=jax.ShapeDtype...  22.3 us
    unnamed x1, local copies, waits for them, and re-layouts  2.29 us

profile of v2, /device:TPU:0, one launch (start us, length us, event | category | flops | bytes accessed | tf_op | source)
XLA Modules:
  0.0 24.6 jit_solution(13396329907827235550)
XLA Ops:
  0.0 22.3 %shard_map.82 = bf16[128,4096]{1,0:T(8,128)(2,1)} custom-call(bf16[128,4096]{1,0:T(8,128)(2,1)} %bitcast.8, bf16[128,4096]{1,0:T(8,128)(2,1)} %bitcast.9, bf16[128,4096]{1,0:T(8,128)(2,1)} %bitcast.10, f32[16,1024]{1,0:T(8,128)} %bitcast.11, f32[16,1024]{1,0:T(8,128)} %bitcast.12, f32[1,1024]{1,0:T(1,128)} %bitcast.13, ...), custom_call_target="tpu_custom_call" | custom-call | tf_op jit(solution)/shard_map/pallas_call | solution.py:362
  22.3 2.3 %copy.10 = bf16[1,128,4096]{2,1,0:T(8,128)(2,1)} copy(bf16[1,128,4096]{2,1,0:T(8,128)(2,1)} %bitcast.7) | data formatting | bytes 2097152

commit v3 on v2

--- a/solution.py
+++ b/solution.py
@@ -12,6 +12,7 @@
 
 MESH = pl.DeviceIdType.MESH
 LANES = 128
+UNROLL = 16
 
 
 def transforms(block):
@@ -25,10 +26,10 @@
 
 def kernel(
     sizes,
-    q_hbm, k_hbm, v_hbm, rates_hbm, residues_hbm, skip_hbm, fwd_hbm, inv_hbm,
+    k_hbm, v_hbm, rates_hbm, residues_hbm, skip_hbm, fwd_hbm, inv_hbm,
     out_hbm,
-    rates_ref, residues_ref, kb, vb, mixs, mixf, qf, outb, par, skp, taps, conv, fwd, inv, statef, states, staten,
-    in_sem, q_sem, mix_sem, par_send, par_recv, skp_send, skp_recv, st_send, st_recv, out_sem,
+    rates_ref, residues_ref, kb, vb, mixs, mixf, outb, par, skp, taps, spec, conv, fwd, inv, statef, states, staten,
+    in_sem, mix_sem, par_send, par_recv, skp_send, skp_recv, st_send, st_recv, out_sem,
 ):
     tokens, half, shard, modes, ctx_size, dp_size, width = sizes
     pairs = ctx_size // 2
@@ -49,7 +50,6 @@
 
     load_k = pltpu.make_async_copy(k_hbm, kb, in_sem.at[0])
     load_v = pltpu.make_async_copy(v_hbm, vb, in_sem.at[1])
-    load_q = pltpu.make_async_copy(q_hbm.at[:, pl.ds(my_cols, half)], qf.at[my_rows, :], in_sem.at[2])
     load_f = pltpu.make_async_copy(fwd_hbm, fwd, in_sem.at[3])
     load_i = pltpu.make_async_copy(inv_hbm, inv, in_sem.at[4])
     slot = dp % half_shards
@@ -68,7 +68,6 @@
     load_v.start()
     load_f.start()
     load_i.start()
-    load_q.start()
 
     barrier = pltpu.get_barrier_semaphore()
     pl.semaphore_signal(barrier, inc=1, device_id={"ctx": mate}, device_id_type=MESH)
@@ -111,10 +110,6 @@
             par_copy(slot, target, step - 1).start()
             skp_copy(slot, target, step - 1).start()
 
-    send_q = pltpu.make_async_remote_copy(
-        src_ref=q_hbm.at[:, pl.ds(mate_cols, half)], dst_ref=qf.at[my_rows, :],
-        send_sem=q_sem.at[0], recv_sem=q_sem.at[1], device_id={"ctx": mate}, device_id_type=MESH,
-    )
     send_mix = pltpu.make_async_remote_copy(
         src_ref=mixs, dst_ref=mixf.at[my_rows, :],
         send_sem=mix_sem.at[0], recv_sem=mix_sem.at[1], device_id={"ctx": mate}, device_id_type=MESH,
@@ -132,7 +127,6 @@
         ).astype(jnp.bfloat16)
 
     send_mix.start()
-    send_q.start()
 
     @pl.loop(0, chunks)
     def _(index):
@@ -142,6 +136,15 @@
             kb[:, src].astype(jnp.float32) * vb[:, src].astype(jnp.float32)
         ).astype(jnp.bfloat16)
 
+    load_f.wait()
+    load_i.wait()
+    send_mix.wait_recv()
+
+    @pl.loop(0, chunks)
+    def _(index):
+        cols = pl.ds(pl.multiple_of(index * width, LANES), width)
+        spec[:, cols] = jnp.dot(fwd[...], mixf[:, cols], preferred_element_type=jnp.float32)
+
     for place in range(half_shards):
         source = core * half_shards + place
 
@@ -149,8 +152,6 @@
         def _():
             par_copy(place, source, 0).wait_recv()
             skp_copy(place, source, 0).wait_recv()
-
-    send_mix.wait_recv()
 
     shard_groups = shard // LANES
     rows8 = lax.broadcasted_iota(jnp.int32, (8, LANES), 0).astype(jnp.float32)
@@ -189,7 +190,7 @@
             spread(start[m : m + 1]) * jnp.exp(-spread(decay[m : m + 1]) * rows8)
             for m in range(modes)
         )
-        lax.fori_loop(0, block // 16, step, powers)
+        lax.fori_loop(0, block // 16, step, powers, unroll=UNROLL)
 
     def state_copy(index, target_pos, source_pos):
         cols = pl.ds(pl.multiple_of(index * width, LANES), width)
@@ -219,7 +220,7 @@
                         return tuple(h * a + both[8:16] for h, a in zip(held, ratios))
 
                     held = tuple(jnp.zeros((8, LANES), jnp.float32) for _ in range(modes))
-                    held = lax.fori_loop(0, block // 16, step, held)
+                    held = lax.fori_loop(0, block // 16, step, held, unroll=UNROLL)
                     for m in range(modes):
                         last = held[m] * jnp.exp(-spread(decay[m : m + 1]) * (7.0 - rows8))
                         statef[m : m + 1, :] = jnp.sum(last, axis=0, keepdims=True)
@@ -230,9 +231,6 @@
                     @pl.when(pos < later)
                     def _():
                         state_copy(index, later, pos).start()
-
-    load_f.wait()
-    load_i.wait()
 
     @pl.loop(0, chunks)
     def _(index):
@@ -250,19 +248,14 @@
             exp_sums(decay, gain, store)
 
         cols = pl.ds(pl.multiple_of(index * width, LANES), width)
-        forward = fwd[...]
-        spec = jnp.dot(forward, mixf[:, cols], preferred_element_type=jnp.float32)
-        filt = jnp.dot(forward, taps[...], preferred_element_type=jnp.float32)
-        sr, si = spec[:block], spec[block:]
+        filt = jnp.dot(fwd[...], taps[...], preferred_element_type=jnp.float32)
+        sr, si = spec[:block, cols], spec[block:, cols]
         fr, fi = filt[:block], filt[block:]
         prod_r = (sr * fr - si * fi).astype(jnp.bfloat16)
         prod_i = (sr * fi + si * fr).astype(jnp.bfloat16)
         conv[:, cols] = jnp.dot(
             inv[:, :block], prod_r, preferred_element_type=jnp.float32
         ) + jnp.dot(inv[:, block:], prod_i, preferred_element_type=jnp.float32)
-
-    load_q.wait()
-    send_q.wait_recv()
 
     def out_copies(index):
         cols = pl.ds(pl.multiple_of(index * width, LANES), width)
@@ -313,10 +306,9 @@
             cols = pl.ds(pl.multiple_of(group * LANES, LANES), LANES)
             place = group // shard_groups
             direct = skp[place, :, pl.ds(pl.multiple_of(group % shard_groups * LANES, LANES), LANES)]
-            outb[:, cols] = (
-                qf[:, cols].astype(jnp.float32)
-                * (conv[:, cols] + direct * mixf[:, cols].astype(jnp.float32))
-            ).astype(jnp.bfloat16)
+            outb[:, cols] = (conv[:, cols] + direct * mixf[:, cols].astype(jnp.float32)).astype(
+                jnp.bfloat16
+            )
 
         local, remote = out_copies(index)
         local.start()
@@ -329,7 +321,6 @@
             par_copy(slot, target, step - 1).wait_send()
             skp_copy(slot, target, step - 1).wait_send()
 
-    send_q.wait_send()
     send_mix.wait_send()
     for index in range(chunks):
         for later in range(1, pairs):
@@ -359,10 +350,10 @@
     slots = max(pairs - 1, 1)
     dma = pltpu.SemaphoreType.DMA
     sizes = (tokens, half, shard, modes, ctx_size, dp_size, width)
-    gated = pl.pallas_call(
+    mixed_out = pl.pallas_call(
         functools.partial(kernel, sizes),
         out_shape=jax.ShapeDtypeStruct((tokens, channels), bf16),
-        in_specs=[hbm_spec] * 8,
+        in_specs=[hbm_spec] * 7,
         out_specs=hbm_spec,
         scratch_shapes=[
             pltpu.VMEM((modes, shard), f32),
@@ -372,10 +363,10 @@
             pltpu.VMEM((tokens, half), bf16),
             pltpu.VMEM((block, half), bf16),
             pltpu.VMEM((block, half), bf16),
-            pltpu.VMEM((block, half), bf16),
             pltpu.VMEM((dp_size // 2, 2, modes, shard), bf16),
             pltpu.VMEM((dp_size // 2, 1, shard), f32),
             pltpu.VMEM((block, width), bf16),
+            pltpu.VMEM((2 * block, half), f32),
             pltpu.VMEM((block, half), f32),
             pltpu.VMEM((2 * block, block), bf16),
             pltpu.VMEM((block, 2 * block), bf16),
@@ -383,7 +374,6 @@
             pltpu.VMEM((modes, half), bf16),
             pltpu.VMEM((slots, modes, half), bf16),
             dma((8,)),
-            dma((2,)),
             dma((2,)),
             dma((dp_size - 1,)),
             dma((dp_size // 2,)),
@@ -397,10 +387,10 @@
             collective_id=0, has_side_effects=True, vmem_limit_bytes=60 * 2**20
         ),
     )(
-        queries[0], keys[0], values[0], rates.T, residues.T, skip[None, :],
+        keys[0], values[0], rates.T, residues.T, skip[None, :],
         jnp.asarray(forward), jnp.asarray(inverse),
     )
-    return gated[None]
+    return (queries.astype(f32) * mixed_out[None].astype(f32)).astype(bf16)
 
 
 def solution(mesh):

time: 24.7 us -> 21.8 us (0.88)
  Pallas kernels: 22.3 us -> 19.2 us
  other arithmetic: 0 us -> 2.45 us
  local copies, waits for them, and re-layouts: 2.29 us -> 0.01 us
    pallas_call x1, Pallas kernels: 22.3 us -> 19.2 us  [body(): pl.pallas_call(functools.partial(kernel, sizes), out_shape=jax.ShapeDtype...]
    convert_element_type x0 -> x1, other arithmetic: none -> 2.45 us  [body(): return (queries.astype(f32) * mixed_out[None].astype(f32)).astype(bf16)]
    unnamed x1 -> x2, local copies, waits for them, and re-layouts: 2.29 us -> 0.01 us
where the time goes in v3:
time: 21.8 us; the launch traced here: 21.7 us
  Pallas kernels  19.2 us (88%)
  other arithmetic  2.45 us (11%)
    pallas_call x1, Pallas kernels, body(): pl.pallas_call(functools.partial(kernel, sizes), out_shape=jax.ShapeDtype...  19.2 us
    convert_element_type x1, other arithmetic, body(): return (queries.astype(f32) * mixed_out[None].astype(f32)).astype(bf16)  2.45 us

profile of v3, /device:TPU:0, one launch (start us, length us, event | category | flops | bytes accessed | tf_op | source)
XLA Modules:
  0.0 21.7 jit_solution(11508710747696576771)
XLA Ops:
  0.0 0.0 copy-start
  0.0 19.2 %shard_map.82 = bf16[128,4096]{1,0:T(8,128)(2,1)} custom-call(bf16[128,4096]{1,0:T(8,128)(2,1)} %bitcast.8, bf16[128,4096]{1,0:T(8,128)(2,1)} %bitcast.9, f32[16,1024]{1,0:T(8,128)} %bitcast.10, f32[16,1024]{1,0:T(8,128)} %bitcast.11, f32[1,1024]{1,0:T(1,128)} %bitcast.12, bf16[512,256]{1,0:T(8,128)(2,1)} %constant.4.clone.fwd_hbm, ...), custom_call_target="tpu_custom_call" | custom-call | tf_op jit(solution)/shard_map/pallas_call | solution.py:353
  19.2 0.0 copy-done
  19.2 2.4 %fusion = bf16[1,128,4096]{2,1,0:T(8,128)(2,1)} fusion(bf16[1,128,4096]{2,1,0:T(8,128)(2,1)S(1)} %copy-done, bf16[128,4096]{1,0:T(8,128)(2,1)} %shard_map.82), kind=kLoop, calls=%fused_computation.1 | loop fusion | flops 2097152 | bytes 3145728 | tf_op jit(solution)/shard_map/convert_element_type | solution.py:393
Async XLA Ops:
  0.0 19.2 %copy-start = (bf16[1,128,4096]{2,1,0:T(8,128)(2,1)S(1)}, bf16[1,128,4096]{2,1,0:T(8,128)(2,1)}, u32[]{:S(2)}) copy-start(bf16[1,128,4096]{2,1,0:T(8,128)(2,1)} %param.8) | copy-start | bytes 3145732

commit v4 on v3

--- a/solution.py
+++ b/solution.py
@@ -167,6 +167,10 @@
             par[place, 1, :, cols].astype(jnp.float32),
         )
 
+    def group_skip(group):
+        cols = pl.ds(pl.multiple_of(group % shard_groups * LANES, LANES), LANES)
+        return skp[group // shard_groups, :, cols]
+
     def tree(parts):
         while len(parts) > 1:
             parts = [
@@ -206,7 +210,7 @@
         def _():
             @pl.loop(0, chunks)
             def _(index):
-                @pl.loop(0, groups)
+                @pl.loop(0, groups, unroll=True)
                 def _(inner):
                     group = index * groups + inner
                     cols = pl.ds(pl.multiple_of(group * LANES, LANES), LANES)
@@ -232,23 +236,20 @@
                     def _():
                         state_copy(index, later, pos).start()
 
-    @pl.loop(0, chunks)
-    def _(index):
-        @pl.loop(0, groups)
-        def _(inner):
-            group = index * groups + inner
-            cols = pl.ds(pl.multiple_of(group * LANES, LANES), LANES)
-            decay, gain = group_params(group)
+    def make_taps(index):
+        for inner in range(groups):
+            decay, gain = group_params(index * groups + inner)
 
             def store(row, sums):
-                taps[pl.ds(row, 16), pl.ds(pl.multiple_of(inner * LANES, LANES), LANES)] = sums.astype(
+                taps[index, pl.ds(row, 16), inner * LANES : (inner + 1) * LANES] = sums.astype(
                     jnp.bfloat16
                 )
 
             exp_sums(decay, gain, store)
 
+    def convolve(index):
         cols = pl.ds(pl.multiple_of(index * width, LANES), width)
-        filt = jnp.dot(fwd[...], taps[...], preferred_element_type=jnp.float32)
+        filt = jnp.dot(fwd[...], taps[index], preferred_element_type=jnp.float32)
         sr, si = spec[:block, cols], spec[block:, cols]
         fr, fi = filt[:block], filt[block:]
         prod_r = (sr * fr - si * fi).astype(jnp.bfloat16)
@@ -257,6 +258,15 @@
             inv[:, :block], prod_r, preferred_element_type=jnp.float32
         ) + jnp.dot(inv[:, block:], prod_i, preferred_element_type=jnp.float32)
 
+    make_taps(0)
+
+    @pl.loop(0, chunks - 1)
+    def _(index):
+        convolve(index)
+        make_taps(index + 1)
+
+    convolve(chunks - 1)
+
     def out_copies(index):
         cols = pl.ds(pl.multiple_of(index * width, LANES), width)
         target = pl.ds(pl.multiple_of(my_cols + index * width, LANES), width)
@@ -280,7 +290,7 @@
 
         @pl.when(pos > 0)
         def _():
-            @pl.loop(0, groups)
+            @pl.loop(0, groups, unroll=True)
             def _(inner):
                 group = index * groups + inner
                 cols = pl.ds(pl.multiple_of(group * LANES, LANES), LANES)
@@ -295,20 +305,25 @@
                     )
                 start = total * gain * jnp.exp(-decay)
 
+                direct = group_skip(group)
+
                 def store(row, sums):
-                    conv[pl.ds(row, 16), cols] += sums
+                    rows = pl.ds(row, 16)
+                    outb[rows, cols] = (
+                        conv[rows, cols] + sums + direct * mixf[rows, cols].astype(jnp.float32)
+                    ).astype(jnp.bfloat16)
 
                 exp_sums(decay, start, store)
 
-        @pl.loop(0, groups)
-        def _(inner):
-            group = index * groups + inner
-            cols = pl.ds(pl.multiple_of(group * LANES, LANES), LANES)
-            place = group // shard_groups
-            direct = skp[place, :, pl.ds(pl.multiple_of(group % shard_groups * LANES, LANES), LANES)]
-            outb[:, cols] = (conv[:, cols] + direct * mixf[:, cols].astype(jnp.float32)).astype(
-                jnp.bfloat16
-            )
+        @pl.when(pos == 0)
+        def _():
+            @pl.loop(0, groups, unroll=True)
+            def _(inner):
+                group = index * groups + inner
+                cols = pl.ds(pl.multiple_of(group * LANES, LANES), LANES)
+                outb[:, cols] = (
+                    conv[:, cols] + group_skip(group) * mixf[:, cols].astype(jnp.float32)
+                ).astype(jnp.bfloat16)
 
         local, remote = out_copies(index)
         local.start()
@@ -365,7 +380,7 @@
             pltpu.VMEM((block, half), bf16),
             pltpu.VMEM((dp_size // 2, 2, modes, shard), bf16),
             pltpu.VMEM((dp_size // 2, 1, shard), f32),
-            pltpu.VMEM((block, width), bf16),
+            pltpu.VMEM((chunks, block, width), bf16),
             pltpu.VMEM((2 * block, half), f32),
             pltpu.VMEM((block, half), f32),
             pltpu.VMEM((2 * block, block), bf16),

time: 21.8 us -> 21 us (0.963)
  Pallas kernels: 19.2 us -> 18.3 us
    pallas_call x1, Pallas kernels: 19.2 us -> 18.3 us  [body(): pl.pallas_call(functools.partial(kernel, sizes), out_shape=jax.ShapeDtype...]
where the time goes in v4:
time: 21 us; the launch traced here: 20.8 us
  Pallas kernels  18.3 us (87%)
  other arithmetic  2.45 us (12%)
    pallas_call x1, Pallas kernels, body(): pl.pallas_call(functools.partial(kernel, sizes), out_shape=jax.ShapeDtype...  18.3 us
    convert_element_type x1, other arithmetic, body(): return (queries.astype(f32) * mixed_out[None].astype(f32)).astype(bf16)  2.45 us

profile of v4, /device:TPU:0, one launch (start us, length us, event | category | flops | bytes accessed | tf_op | source)
XLA Modules:
  0.0 20.8 jit_solution(14397900279386027051)
XLA Ops:
  0.0 0.0 copy-start
  0.0 18.3 %shard_map.82 = bf16[128,4096]{1,0:T(8,128)(2,1)} custom-call(bf16[128,4096]{1,0:T(8,128)(2,1)} %bitcast.8, bf16[128,4096]{1,0:T(8,128)(2,1)} %bitcast.9, f32[16,1024]{1,0:T(8,128)} %bitcast.10, f32[16,1024]{1,0:T(8,128)} %bitcast.11, f32[1,1024]{1,0:T(1,128)} %bitcast.12, bf16[512,256]{1,0:T(8,128)(2,1)} %constant.4.clone.fwd_hbm, ...), custom_call_target="tpu_custom_call" | custom-call | tf_op jit(solution)/shard_map/pallas_call | solution.py:368
  18.4 0.0 copy-done
  18.4 2.4 %fusion = bf16[1,128,4096]{2,1,0:T(8,128)(2,1)} fusion(bf16[1,128,4096]{2,1,0:T(8,128)(2,1)S(1)} %copy-done, bf16[128,4096]{1,0:T(8,128)(2,1)} %shard_map.82), kind=kLoop, calls=%fused_computation.1 | loop fusion | flops 2097152 | bytes 3145728 | tf_op jit(solution)/shard_map/convert_element_type | solution.py:408
Async XLA Ops:
  0.0 18.4 %copy-start = (bf16[1,128,4096]{2,1,0:T(8,128)(2,1)S(1)}, bf16[1,128,4096]{2,1,0:T(8,128)(2,1)}, u32[]{:S(2)}) copy-start(bf16[1,128,4096]{2,1,0:T(8,128)(2,1)} %param.8) | copy-start | bytes 3145732
